TPU v7x, 512 devices: a whole 4x8x8 slice. The times are simulated.
512 devices in a mesh: dp: 32 (over x, z), seq: 16 (over y, core).
Axes of the slice: x: 4, y: 8, z: 8, core: 2. Of those that a mesh axis runs over, the one named last changes fastest.
Arguments:
- queries: bfloat16 [65536, 1024], P(('dp', 'seq')), parts along dimension 0, may hold values from -6 to 6
- keyvals: bfloat16 [524288, 8, 128], P(('dp', 'seq')), parts along dimension 0, may hold values from -16 to 16
- residual: bfloat16 [65536, 1024], P(('dp', 'seq')), parts along dimension 0, may hold values from -16 to 16
- out_weight: bfloat16 [1024, 1024], P('seq'), may hold values from -0.1875 to 0.1875
- norm_gain: float32 [1024], replicated, may hold values from 0.25 to 1.75
- expert_up: bfloat16 [16, 1024, 512], P('seq'), may hold values from -0.1875 to 0.1875
- expert_down: bfloat16 [16, 256, 1024], P('seq'), may hold values from -0.375 to 0.375
- expert_ids: int32 [65536, 8], P(('dp', 'seq')), parts along dimension 0, may hold values from 0 to 15, as said below
- slot_index: int32 [65536, 8], P(('dp', 'seq')), parts along dimension 0, may hold values from 0 to 79, as said below
- gate_weights: float32 [65536, 8], P(('dp', 'seq')), parts along dimension 0, may hold values from 0.05 to 0.5
Outputs:
- layer_out: bfloat16 [65536, 1024], P(('dp', 'seq')), parts along dimension 0
There are 32 independent parts, one for each index of `dp`. A program takes and returns all parts, laid end to end along the dimension named above; an argument that names none is the same for every part. Nothing has to cross between parts.
Inputs may be any that keep to these rules, and one draw needn't show every extreme that they name: `expert_ids`: each row names 8 different experts. Among the 128 rows of one device no expert is named by more than 80 rows, and in every draw one expert is named by exactly 80 rows on every device. `slot_index`: rows of one device that name the same expert have different slots.
All inputs are finite; a program needn't handle non-finite values.
Results may differ from a plain program's by a relative error of at most 0.014.
Values may be sent and summed in bfloat16 or wider, within the bound.
A program may use at most 64 MiB of HBM per device.

v0:
```python
import jax
import jax.numpy as jnp
from jax import lax
from jax.sharding import PartitionSpec as P

HEADS = 16
HEAD = 64
EXPERTS = 16
FF = 256
CAP = 80


MASKED = -1e30


def attend(query_heads, key_values, query_rows, shard_len):
    query_count, heads_here, head_size = query_heads.shape
    query_tile = 512
    key_tile = 512
    score_scale = head_size ** (-0.5)
    row_ids = jnp.arange(query_count)
    query_pos = row_ids // query_rows * shard_len + row_ids % query_rows

    def query_step(tile_index, result):
        row_start = tile_index * query_tile
        tile_query = lax.dynamic_slice_in_dim(query_heads, row_start, query_tile, 0)
        tile_pos = lax.dynamic_slice_in_dim(query_pos, row_start, query_tile, 0)
        last_row = row_start + query_tile - 1
        last_pos = last_row // query_rows * shard_len + last_row % query_rows
        key_tiles = last_pos // key_tile + 1

        def key_step(key_index, running):
            highest, totals, summed = running
            tile_keys = lax.dynamic_slice_in_dim(key_values, key_index * key_tile, key_tile, 0)
            scores = (
                jnp.einsum(
                    "qhd,khd->hqk",
                    tile_query,
                    tile_keys[..., :head_size],
                    preferred_element_type=jnp.float32,
                )
                * score_scale
            )
            key_pos = key_index * key_tile + jnp.arange(key_tile)
            scores = jnp.where(key_pos[None, None, :] <= tile_pos[None, :, None], scores, MASKED)
            newest = jnp.maximum(highest, jnp.max(scores, axis=-1))
            shrink = jnp.exp(highest - newest)
            weights = jnp.exp(scores - newest[..., None])
            totals = totals * shrink + jnp.sum(weights, axis=-1)
            summed = summed * shrink[..., None] + jnp.einsum(
                "hqk,khd->hqd",
                weights.astype(jnp.bfloat16),
                tile_keys[..., head_size:],
                preferred_element_type=jnp.float32,
            )
            return (newest, totals, summed)

        start_state = (
            jnp.full((heads_here, query_tile), MASKED, jnp.float32),
            jnp.zeros((heads_here, query_tile), jnp.float32),
            jnp.zeros((heads_here, query_tile, head_size), jnp.float32),
        )
        highest, totals, summed = lax.fori_loop(0, key_tiles, key_step, start_state)
        context = (summed / totals[..., None]).astype(jnp.bfloat16).transpose(1, 0, 2)
        return lax.dynamic_update_slice_in_dim(result, context, row_start, 0)

    blank_out = jnp.zeros((query_count, heads_here, head_size), jnp.bfloat16)
    return lax.fori_loop(0, query_count // query_tile, query_step, blank_out)


def body(
    queries,
    keyvals,
    residual,
    out_weight,
    norm_gain,
    expert_up,
    expert_down,
    expert_ids,
    slot_index,
    gate_weights,
):
    devices = lax.axis_size("seq")
    query_rows = queries.shape[0]
    shard_len = keyvals.shape[0]
    group_heads = keyvals.shape[1]
    heads_here = HEADS // devices
    head_major = lax.all_to_all(queries, "seq", split_axis=1, concat_axis=0, tiled=True)
    query_heads = head_major.reshape(devices * query_rows, heads_here, HEAD)
    repeated = jnp.repeat(keyvals, HEADS // group_heads, axis=1)
    key_values = lax.all_to_all(repeated, "seq", split_axis=1, concat_axis=0, tiled=True)
    context = attend(query_heads, key_values, query_rows, shard_len)
    token_major = lax.all_to_all(
        context.reshape(devices * query_rows, heads_here * HEAD),
        "seq",
        split_axis=0,
        concat_axis=1,
        tiled=True,
    )
    summed_out = residual.astype(jnp.float32) + jnp.dot(
        token_major,
        lax.all_gather(out_weight, "seq", axis=0, tiled=True),
        preferred_element_type=jnp.float32,
    )
    hidden = summed_out.astype(jnp.bfloat16)
    widened = lax.optimization_barrier(hidden).astype(jnp.float32)
    normed = (
        widened * lax.rsqrt(jnp.mean(widened * widened, axis=-1, keepdims=True) + 1e-05) * norm_gain
    ).astype(jnp.bfloat16)
    feature_width = normed.shape[1]
    target = expert_ids * CAP + slot_index
    chooser = jnp.any(jnp.arange(EXPERTS * CAP)[:, None, None] == target[None], axis=2).astype(
        jnp.bfloat16
    )
    outgoing = jnp.dot(chooser, normed, preferred_element_type=jnp.float32).astype(jnp.bfloat16)
    outgoing = outgoing.reshape(EXPERTS, 1, CAP, feature_width)
    arrived = lax.all_to_all(outgoing, "seq", split_axis=0, concat_axis=1, tiled=True)
    local_count, sources, item_count, arrived_width = arrived.shape
    flat_rows = arrived.reshape(local_count, sources * item_count, arrived_width)
    projected = jnp.einsum("erd,edf->erf", flat_rows, expert_up, preferred_element_type=jnp.float32)
    activated = (jax.nn.silu(projected[..., :FF]) * projected[..., FF:]).astype(jnp.bfloat16)
    produced = jnp.einsum(
        "erf,efd->erd", activated, expert_down, preferred_element_type=jnp.float32
    ).astype(jnp.bfloat16)
    produced = produced.reshape(local_count, sources, item_count, arrived_width)
    returned = lax.all_to_all(produced, "seq", split_axis=1, concat_axis=0, tiled=True)
    flat_back = returned.reshape(EXPERTS * CAP, feature_width)
    picked = jnp.take(flat_back, target, axis=0)
    mixture = jnp.zeros((query_rows, feature_width), jnp.float32)
    for choice_index in range(picked.shape[1]):
        mixture = mixture + gate_weights[:, choice_index : choice_index + 1] * picked[
            :, choice_index
        ].astype(jnp.float32)
    return (widened + mixture).astype(jnp.bfloat16)


def solution(mesh):
    placed = (
        P(("dp", "seq"), None),
        P(("dp", "seq"), None, None),
        P(("dp", "seq"), None),
        P("seq", None),
        P(),
        P("seq", None, None),
        P("seq", None, None),
        P(("dp", "seq"), None),
        P(("dp", "seq"), None),
        P(("dp", "seq"), None),
    )
    return jax.shard_map(
        body, mesh=mesh, in_specs=placed, out_specs=P(("dp", "seq"), None), check_vma=False
    )
```

profile of v0, /device:TPU:1, one launch (start us, length us, event | category | flops | bytes accessed | tf_op | source)
XLA Modules:
  0.0 518.2 jit_solution(12162442988193045875)
XLA Ops:
  6.5 1.9 copy.39
  8.4 10.2 %all-to-all-start = ((bf16[128,16,64]{0,2,1:T(8,128)(2,1)}), bf16[128,16,64]{0,2,1:T(8,128)(2,1)S(1)}, u32[]{:S(2)}, u32[]{:S(2)}) async-start(bf16[128,16,64]{0,2,1:T(8,128)(2,1)} %bitcast.11), calls=%async_computation | async-start | bytes 524288 | tf_op jit(solution)/shard_map/all_to_all | solution.py:88
  18.6 1.9 copy.41
  20.5 10.0 %all-to-all-done = bf16[128,16,64]{0,2,1:T(8,128)(2,1)S(1)} async-done(((bf16[128,16,64]{0,2,1:T(8,128)(2,1)}), bf16[128,16,64]{0,2,1:T(8,128)(2,1)S(1)}, u32[]{:S(2)}, u32[]{:S(2)}) %all-to-all-start) | async-done | bytes 262176 | tf_op jit(solution)/shard_map/all_to_all | solution.py:88
  30.5 2.8 broadcast_in_dim.34
  33.2 4.4 all-to-all-start.1
  38.7 101.6 %all-to-all-done.1 = bf16[1024,16,128]{2,0,1:T(8,128)(2,1)} async-done(((bf16[1024,16,128]{2,0,1:T(8,128)(2,1)}), bf16[1024,16,128]{2,0,1:T(8,128)(2,1)}, u32[]{:S(2)}, u32[]{:S(2)}) %all-to-all-start.1) | async-done | bytes 4194336 | tf_op jit(solution)/shard_map/all_to_all | solution.py:91
  140.4 6.4 %copy.42 = bf16[16384,1,128]{0,2,1:T(8,128)(2,1)} copy(bf16[16384,1,128]{2,0,1:T(8,128)(2,1)} %bitcast.16) | data formatting | bytes 8388608 | tf_op jit(solution)/shard_map/while | solution.py:68
  146.9 200.7 %while.77 = (s32[]{:T(128)}, bf16[2048,1,64]{0,2,1:T(8,128)(2,1)S(1)}, bf16[2048,1,64]{0,2,1:T(8,128)(2,1)S(1)}, s32[2048]{0:T(1024)S(1)}, bf16[16384,1,128]{0,2...) while((s32[]{:T(128)}, ...), condition=%wide.region_5.6_spmd, body=%wide.region_0.5_spmd.sunk | while | flops 69338664 | bytes 4113355 | solution.py:68
  147.1 18.4 %while.78 = (s32[]{:T(128)}, f32[1,512]{1,0:T(1,128)S(1)}, f32[1,512]{1,0:T(1,128)S(1)}, f32[1,512,64]{1,2,0:T(8,128)S(1)}, s32[]{:T(128)}, /*index=5*/s32[512]{...) while((s32[]{:T(128)}, f32[1,512]{1,0:T(1,128)S(1)}, ...), condition=%wide.region_4.4_spmd, body=%wide.region_1.3_spmd.sunk | while | flops 69273088 | bytes 3643591 | solution.py:63
  147.1 1.2 fusion.51
  149.7 1.2 fusion.51
  152.4 1.2 fusion.51
  155.0 1.2 fusion.51
  160.2 1.2 fusion.51
  162.9 1.2 fusion.51
  165.7 39.4 %while.78 = (s32[]{:T(128)}, f32[1,512]{1,0:T(1,128)S(1)}, f32[1,512]{1,0:T(1,128)S(1)}, f32[1,512,64]{1,2,0:T(8,128)S(1)}, s32[]{:T(128)}, /*index=5*/s32[512]{...) while((s32[]{:T(128)}, f32[1,512]{1,0:T(1,128)S(1)}, ...), condition=%wide.region_4.4_spmd, body=%wide.region_1.3_spmd.sunk | while | flops 69273088 | bytes 3643591 | solution.py:63
  165.7 1.2 fusion.51
  168.4 1.2 fusion.51
  171.0 1.2 fusion.51
  173.6 1.2 fusion.51
  176.3 1.2 fusion.51
  178.9 1.2 fusion.51
  181.5 1.2 fusion.51
  184.1 1.2 fusion.51
  186.8 1.2 fusion.51
  189.4 1.2 fusion.51
  194.6 1.2 fusion.51
  197.3 1.2 fusion.51
  199.9 1.2 fusion.51
  205.4 60.4 %while.78 = (s32[]{:T(128)}, f32[1,512]{1,0:T(1,128)S(1)}, f32[1,512]{1,0:T(1,128)S(1)}, f32[1,512,64]{1,2,0:T(8,128)S(1)}, s32[]{:T(128)}, /*index=5*/s32[512]{...) while((s32[]{:T(128)}, f32[1,512]{1,0:T(1,128)S(1)}, ...), condition=%wide.region_4.4_spmd, body=%wide.region_1.3_spmd.sunk | while | flops 69273088 | bytes 3643591 | solution.py:63
  205.4 1.2 fusion.51
  208.0 1.2 fusion.51
  266.1 81.5 %while.78 = (s32[]{:T(128)}, f32[1,512]{1,0:T(1,128)S(1)}, f32[1,512]{1,0:T(1,128)S(1)}, f32[1,512,64]{1,2,0:T(8,128)S(1)}, s32[]{:T(128)}, /*index=5*/s32[512]{...) while((s32[]{:T(128)}, f32[1,512]{1,0:T(1,128)S(1)}, ...), condition=%wide.region_4.4_spmd, body=%wide.region_1.3_spmd.sunk | while | flops 69273088 | bytes 3643591 | solution.py:63
  266.1 1.2 fusion.51
  268.7 1.2 fusion.51
  348.4 5.4 %all-to-all-start.2 = ((bf16[16,128,64]{1,2,0:T(8,128)(2,1)}), bf16[16,128,64]{1,2,0:T(8,128)(2,1)S(1)}, u32[]{:S(2)}, u32[]{:S(2)}) async-start(bf16[16,128,64]{1,2,0:T(8,128)(2,1)} %copy.43), calls=%async_computation.2 | async-start | bytes 524288 | tf_op jit(solution)/shard_map/all_to_all | solution.py:93
  353.8 4.6 fusion.10
  358.5 7.0 %all-to-all-done.2 = bf16[16,128,64]{1,2,0:T(8,128)(2,1)S(1)} async-done(((bf16[16,128,64]{1,2,0:T(8,128)(2,1)}), bf16[16,128,64]{1,2,0:T(8,128)(2,1)S(1)}, u32[]{:S(2)}, u32[]{:S(2)}) %all-to-all-start.2) | async-done | bytes 262176 | tf_op jit(solution)/shard_map/all_to_all | solution.py:93
  365.5 2.1 fusion.12
  368.6 65.0 %all_to_all.71 = bf16[16,1,80,1024]{3,2,1,0:T(8,128)(2,1)S(1)} all-to-all(bf16[16,1,80,1024]{3,2,1,0:T(8,128)(2,1)S(1)} %bitcast.149), channel_id=1, replica_groups=mesh['dp'=32,'seq'=16] {'seq'}, dimensions={0} | all-to-all | bytes 5242880 | tf_op jit(solution)/shard_map/all_to_all | solution.py:117
  433.6 1.5 convolution_bitcast_fusion.1
  435.1 2.4 convolution_convert_fusion
  437.5 4.7 all-to-all-start.4
  442.4 58.2 %all-to-all-done.4 = bf16[1,16,80,1024]{3,2,0,1:T(8,128)(2,1)} async-done(((bf16[1,16,80,1024]{3,2,0,1:T(8,128)(2,1)}), bf16[1,16,80,1024]{3,2,0,1:T(8,128)(2,1)}, u32[]{:S(2)}, u32[]{:S(2)}) %all-to-all-start.4) | async-done | bytes 2621472 | tf_op jit(solution)/shard_map/all_to_all | solution.py:126
  500.6 7.1 %gather_fusion = bf16[1024,1024]{1,0:T(8,128)(2,1)S(1)} fusion(bf16[1280,1024]{1,0:T(8,128)(2,1)} %bitcast.29, s32[1024]{0:T(1024)S(1)} %broadcast_clamp_fusion), kind=kCustom, calls=%fused_computation | custom fusion | bytes 4198400 | tf_op jit(solution)/shard_map/jit(_take)/gather | solution.py:128
  507.7 2.5 copy_select_fusion
  510.1 1.2 fusion.19
  (565 shorter events, 171.7 us)
Async XLA Ops:
  6.5 427.0 %copy-start = (bf16[1,1024,512]{2,1,0:T(8,128)(2,1)S(1)}, bf16[1,1024,512]{2,1,0:T(8,128)(2,1)}, u32[]{:S(2)}) copy-start(bf16[1,1024,512]{2,1,0:T(8,128)(2,1)} %param.19) | copy-start | bytes 3145732
  8.4 22.1 %all-to-all-start = ((bf16[128,16,64]{0,2,1:T(8,128)(2,1)}), bf16[128,16,64]{0,2,1:T(8,128)(2,1)S(1)}, u32[]{:S(2)}, u32[]{:S(2)}) async-start(bf16[128,16,64]{0,2,1:T(8,128)(2,1)} %bitcast.11), calls=%async_computation | async-start | bytes 524288 | tf_op jit(solution)/shard_map/all_to_all | solution.py:88
  33.2 107.1 %all-to-all-start.1 = ((bf16[1024,16,128]{2,0,1:T(8,128)(2,1)}), bf16[1024,16,128]{2,0,1:T(8,128)(2,1)}, u32[]{:S(2)}, u32[]{:S(2)}) async-start(bf16[1024,16,128]{2,0,1:T(8,128)(2,1)} %bitcast.148), calls=%async_computation.1 | async-start | bytes 8388608 | tf_op jit(solution)/shard_map/all_to_all | solution.py:91
  37.7 320.8 %all-gather.2.cloned.1.call-start = ((), (), s32[]{:S(2)}) async-start(), calls=%async_computation.5 | async-start | bytes 2228224 | tf_op jit(solution)/shard_map/all_gather | solution.py:102
  146.8 206.9 %copy-start.3 = (s32[128,8]{0,1:T(8,128)S(1)}, s32[128,8]{0,1:T(8,128)}, u32[]{:S(2)}) copy-start(s32[128,8]{0,1:T(8,128)} %param.22) | copy-start | bytes 12292
  146.8 206.9 %copy-start.4 = (s32[128,8]{0,1:T(8,128)S(1)}, s32[128,8]{0,1:T(8,128)}, u32[]{:S(2)}) copy-start(s32[128,8]{0,1:T(8,128)} %param.21) | copy-start | bytes 12292
  146.8 218.6 %copy-start.1 = (bf16[128,1024]{1,0:T(8,128)(2,1)S(1)}, bf16[128,1024]{1,0:T(8,128)(2,1)}, u32[]{:S(2)}) copy-start(bf16[128,1024]{1,0:T(8,128)(2,1)} %param.16) | copy-start | bytes 786436
  347.6 20.1 %copy-start.2 = (f32[1024]{0:T(1024)S(1)}, f32[1024]{0:T(1024)}, u32[]{:S(2)}) copy-start(f32[1024]{0:T(1024)} %param.18) | copy-start | bytes 12292
  348.4 17.1 %all-to-all-start.2 = ((bf16[16,128,64]{1,2,0:T(8,128)(2,1)}), bf16[16,128,64]{1,2,0:T(8,128)(2,1)S(1)}, u32[]{:S(2)}, u32[]{:S(2)}) async-start(bf16[16,128,64]{1,2,0:T(8,128)(2,1)} %copy.43), calls=%async_computation.2 | async-start | bytes 524288 | tf_op jit(solution)/shard_map/all_to_all | solution.py:93
  433.6 1.5 copy-start.6
  437.5 4.9 copy-start.5
  437.5 63.1 %all-to-all-start.4 = ((bf16[1,16,80,1024]{3,2,0,1:T(8,128)(2,1)}), bf16[1,16,80,1024]{3,2,0,1:T(8,128)(2,1)}, u32[]{:S(2)}, u32[]{:S(2)}) async-start(bf16[1,16,80,1024]{3,2,0,1:T(8,128)(2,1)} %bitcast.153), calls=%async_computation.4 | async-start | bytes 5242880 | tf_op jit(solution)/shard_map/all_to_all | solution.py:126
Sparse Core Ops, SparseCore 0:
  40.6 75.0 all-gather.1
where the time goes:
time: 526 us; the launch traced here: 518 us
  matrix products  185 us (35%)
  waiting for transfers between devices  177 us (34%)
  blocking collectives  65 us (12%)
  other arithmetic  25.7 us (5%)
  starting transfers between devices  24.7 us (5%)
  local copies, waits for them, and re-layouts  22 us (4%)
  between operations  13.6 us (3%)
    all_to_all x1, waiting for transfers between devices, body(): lax.all_to_all(repeated, 'seq', split_axis=1, concat_axis=0, tiled=True)  102 us
    dot_general x76, matrix products, key_step(): jnp.einsum('qhd,khd->hqk', tile_query, tile_keys[..., :head_size], prefer...  89.9 us
    dot_general x76, matrix products, key_step(): jnp.einsum('hqk,khd->hqd', weights.astype(jnp.bfloat16), tile_keys[..., h...  87.9 us
    all_to_all x1, blocking collectives, body(): lax.all_to_all(outgoing, 'seq', split_axis=0, concat_axis=1, tiled=True)  65 us
    all_to_all x1, waiting for transfers between devices, body(): lax.all_to_all(produced, 'seq', split_axis=1, concat_axis=0, tiled=True)  58.2 us
    reduce_sum x76, other arithmetic, key_step(): totals = totals * shrink + jnp.sum(weights, axis=-1)  15 us
  transfers between devices with their start and end apart: 5, of which 4 were waited for; matrix products, arithmetic and copies ran while one was open for 41% of the time, Pallas kernels for 0%

commit v1 on v0

v1 whole, which is shorter than its diff:
```python
import functools

import jax
import jax.numpy as jnp
from jax import lax
from jax.experimental import pallas as pl
from jax.experimental.pallas import tpu as pltpu
from jax.sharding import PartitionSpec as P

CHIPS = 8
ROWS = 128
KEYS = 1024
HEAD = 64
FF = 256
LOW = -1e30
MESH = pl.DeviceIdType.MESH
OFFSETS = (1, 7, 2, 6, 3, 5, 4)


def send(src, dst, send_sem, recv_sem, **where):
    return pltpu.make_async_remote_copy(
        src_ref=src,
        dst_ref=dst,
        send_sem=send_sem,
        recv_sem=recv_sem,
        device_id=where,
        device_id_type=MESH,
    )


def chip_columns(chip):
    return pl.ds(pl.multiple_of(chip * 128, 128), 128)


def attend_kernel(
    kv, q, out,
    kvland, qland, qpad, vt, acc, top, mland, cbuf, cland,
    own_sem, kv_s, kv_r, q_s, q_r, f_s, f_r, m_s, m_r, c_s, c_r,
):
    s = lax.axis_index("seq")
    c = s // 2
    k = lax.rem(s, 2)
    sib = s + 1 - 2 * k

    def chip(d):
        return lax.rem(c + d, CHIPS)

    def peer(d):
        return chip(d) * 2 + k

    barrier = pltpu.get_barrier_semaphore()
    for d in OFFSETS:
        pl.semaphore_signal(barrier, inc=1, device_id={"seq": peer(d)}, device_id_type=MESH)
    pl.semaphore_signal(barrier, inc=1, device_id={"seq": sib}, device_id_type=MESH)
    own_kv = pltpu.make_async_copy(kv.at[c], kvland.at[0], own_sem)
    own_kv.start()
    qland[s] = q[:, chip_columns(c)]
    pl.semaphore_wait(barrier, CHIPS)

    q_out = {d: send(q.at[:, chip_columns(chip(d))], qland.at[s], q_s.at[d], q_r.at[d], seq=peer(d)) for d in OFFSETS}
    kv_out = {d: send(kv.at[chip(d)], kvland.at[d], kv_s.at[d], kv_r.at[d], seq=peer(d)) for d in OFFSETS}
    for d in OFFSETS:
        q_out[d].start()
    q_on = {0: send(qland.at[s], qland.at[s], f_s.at[0], f_r.at[0], seq=sib)}
    q_on[0].start()
    for d in OFFSETS:
        kv_out[d].start()

    acc[...] = jnp.zeros_like(acc)
    top[...] = jnp.full_like(top, LOW)
    vt[HEAD:, :] = jnp.ones((16, KEYS), jnp.bfloat16)

    for d in OFFSETS:
        q_out[d].wait_recv()
        t = peer(CHIPS - d)
        q_on[d] = send(qland.at[t], qland.at[t], f_s.at[d], f_r.at[d], seq=sib)
        q_on[d].start()
    for d in (0,) + OFFSETS:
        q_on[d].wait_recv()

    def prepare(t, carry):
        x = qland[t].astype(jnp.float32) * (HEAD**-0.5)
        first = lax.broadcasted_iota(jnp.int32, (ROWS, 128), 1) < HEAD
        qpad[t, 0:ROWS, :] = jnp.where(first, x, 0.0).astype(jnp.bfloat16)
        qpad[t, ROWS:, :] = jnp.where(first, pltpu.roll(x, HEAD, 1), 0.0).astype(jnp.bfloat16)
        return carry

    lax.fori_loop(0, 2 * CHIPS, prepare, 0)

    def fold(i, scores, values, mask=None):
        if mask is not None:
            scores = jnp.where(mask, scores, LOW)
        old = top[i]
        new = jnp.maximum(old, jnp.max(scores, axis=0, keepdims=True))
        probs = jnp.exp(scores - new)
        if mask is not None:
            probs = jnp.where(mask, probs, 0.0)
        acc[i] = acc[i] * jnp.exp(old - new) + jnp.dot(
            values, probs.astype(jnp.bfloat16), preferred_element_type=jnp.float32
        )
        top[i] = new

    def place(t):
        return lax.rem(t, 2) * CHIPS + t // 2

    def score(keys, t):
        return lax.dot_general(keys, qpad[t], (((1,), (1,)), ((), ())), preferred_element_type=jnp.float32)

    def process(d):
        source = peer(CHIPS - d) if d else s
        for r in range(0, KEYS, 128):
            block = jnp.transpose(kvland[d, r : r + 128, :].astype(jnp.float32))
            vt[0:HEAD, r : r + 128] = block[HEAD:, :].astype(jnp.bfloat16)
        key_row = lax.broadcasted_iota(jnp.int32, (ROWS, 2 * ROWS), 0)
        query_row = lax.rem(lax.broadcasted_iota(jnp.int32, (ROWS, 2 * ROWS), 1), ROWS)
        fold(place(source), score(kvland[d, 0:ROWS, :], source), vt[:, 0:ROWS], key_row <= query_row)

        def step(t, carry):
            fold(place(t), score(kvland[d], t), vt[...])
            return carry

        lax.fori_loop(source + 1, 2 * CHIPS, step, 0)

    own_kv.wait()
    process(0)
    for d in OFFSETS:
        kv_out[d].wait_recv()
        process(d)

    def note(i, carry):
        acc[i, 72:80, :] = jnp.broadcast_to(top[i], (8, 2 * ROWS))
        return carry

    lax.fori_loop(0, 2 * CHIPS, note, 0)
    halves = pl.ds(pl.multiple_of((1 - k) * CHIPS, CHIPS), CHIPS)
    swap = send(acc.at[halves], mland, m_s, m_r, seq=sib)
    swap.start()
    swap.wait_recv()

    def finish(i):
        mine, theirs = acc[k * CHIPS + i], mland[i]
        ma, mb = mine[72:73], theirs[72:73]
        both = jnp.maximum(ma, mb)
        wa, wb = jnp.exp(ma - both), jnp.exp(mb - both)
        merged = mine * wa + theirs * wb
        ctx = merged[0:HEAD] / merged[HEAD : HEAD + 1]
        ctx = jnp.concatenate([ctx[:, 0:ROWS], ctx[:, ROWS:]], axis=0)
        return jnp.transpose(ctx).astype(jnp.bfloat16)

    c_out = {}
    for d in OFFSETS:
        cbuf[d] = finish(chip(d))
        c_out[d] = send(cbuf.at[d], cland.at[:, chip_columns(c)], c_s.at[d], c_r.at[d], seq=peer(d))
        c_out[d].start()
    cland[:, chip_columns(c)] = finish(c)
    for d in OFFSETS:
        c_out[d].wait_recv()
    out[...] = cland[...]
    for d in OFFSETS:
        q_out[d].wait_send()
        kv_out[d].wait_send()
        q_on[d].wait_send()
        c_out[d].wait_send()
    q_on[0].wait_send()
    swap.wait_send()


def attend(kv, q):
    dma = pltpu.SemaphoreType.DMA
    vmem = pl.BlockSpec(memory_space=pltpu.VMEM)
    return pl.pallas_call(
        attend_kernel,
        out_shape=jax.ShapeDtypeStruct((ROWS, 1024), jnp.bfloat16),
        in_specs=[vmem, vmem],
        out_specs=vmem,
        scratch_shapes=[
            pltpu.VMEM((CHIPS, KEYS, 128), jnp.bfloat16),
            pltpu.VMEM((2 * CHIPS, ROWS, 128), jnp.bfloat16),
            pltpu.VMEM((2 * CHIPS, 2 * ROWS, 128), jnp.bfloat16),
            pltpu.VMEM((HEAD + 16, KEYS), jnp.bfloat16),
            pltpu.VMEM((2 * CHIPS, HEAD + 16, 2 * ROWS), jnp.float32),
            pltpu.VMEM((2 * CHIPS, 1, 2 * ROWS), jnp.float32),
            pltpu.VMEM((CHIPS, HEAD + 16, 2 * ROWS), jnp.float32),
            pltpu.VMEM((CHIPS, ROWS, 128), jnp.bfloat16),
            pltpu.VMEM((ROWS, 1024), jnp.bfloat16),
            dma, dma((CHIPS,)), dma((CHIPS,)), dma((CHIPS,)), dma((CHIPS,)), dma((CHIPS,)), dma((CHIPS,)),
            dma, dma, dma((CHIPS,)), dma((CHIPS,)),
        ],
        compiler_params=pltpu.CompilerParams(
            collective_id=0, has_side_effects=True, vmem_limit_bytes=32 * 1024 * 1024
        ),
        cost_estimate=pl.CostEstimate(flops=60_000_000_000, bytes_accessed=100_000_000, transcendentals=16_000_000),
    )(kv, q)


def experts_kernel(ctx, residual, proj, gain, gates, sib_gates, up, down, out, xboth, ysib, yland, x_s, x_r, y_s, y_r):
    s = lax.axis_index("seq")
    k = lax.rem(s, 2)
    sib = s + 1 - 2 * k
    barrier = pltpu.get_barrier_semaphore()
    pl.semaphore_signal(barrier, inc=1, device_id={"seq": sib}, device_id_type=MESH)
    hidden = (
        residual[...].astype(jnp.float32) + jnp.dot(ctx[...], proj[...], preferred_element_type=jnp.float32)
    ).astype(jnp.bfloat16)
    wide = hidden.astype(jnp.float32)
    normed = wide * lax.rsqrt(jnp.mean(wide * wide, axis=-1, keepdims=True) + 1e-05) * gain[...]
    xboth[0:ROWS, :] = normed.astype(jnp.bfloat16)
    pl.semaphore_wait(barrier, 1)
    swap = send(xboth.at[pl.ds(0, ROWS)], xboth.at[pl.ds(ROWS, ROWS)], x_s, x_r, seq=sib)
    swap.start()
    swap.wait()
    x = xboth[...]
    weights = jnp.concatenate([gates[...], sib_gates[...]], axis=0)
    column = lax.broadcasted_iota(jnp.int32, weights.shape, 1)
    total = jnp.zeros((2 * ROWS, 1024), jnp.float32)
    for j in range(CHIPS):
        projected = jnp.dot(x, up[:, j].reshape(1024, 512), preferred_element_type=jnp.float32)
        gate, lift = projected[:, :FF], projected[:, FF:]
        scale = jnp.sum(jnp.where(column == 2 * j + k, weights, 0.0), axis=1, keepdims=True)
        act = (gate / (1.0 + jnp.exp(-gate)) * lift * scale).astype(jnp.bfloat16)
        low = down[0:16, j].reshape(FF, 512)
        high = down[16:32, j].reshape(FF, 512)
        total = total + jnp.concatenate(
            [
                jnp.dot(act, low, preferred_element_type=jnp.float32),
                jnp.dot(act, high, preferred_element_type=jnp.float32),
            ],
            axis=1,
        )
    ysib[...] = total[ROWS:, :]
    back = send(ysib, yland, y_s, y_r, seq=sib)
    back.start()
    back.wait()
    out[...] = (wide + total[0:ROWS, :] + yland[...]).astype(jnp.bfloat16)


def experts(*args):
    dma = pltpu.SemaphoreType.DMA
    vmem = pl.BlockSpec(memory_space=pltpu.VMEM)
    return pl.pallas_call(
        experts_kernel,
        out_shape=jax.ShapeDtypeStruct((ROWS, 1024), jnp.bfloat16),
        in_specs=[vmem] * 8,
        out_specs=vmem,
        scratch_shapes=[
            pltpu.VMEM((2 * ROWS, 1024), jnp.bfloat16),
            pltpu.VMEM((ROWS, 1024), jnp.float32),
            pltpu.VMEM((ROWS, 1024), jnp.float32),
            dma, dma, dma, dma,
        ],
        compiler_params=pltpu.CompilerParams(
            collective_id=1, has_side_effects=True, vmem_limit_bytes=40 * 1024 * 1024
        ),
    )(*args)


def body(
    queries, keyvals, residual, out_weight, norm_gain, expert_up, expert_down, expert_ids, slot_index, gate_weights
):
    dp = lax.axis_index("dp")
    core = lax.rem(lax.axis_index("seq"), 2)
    up_part = lax.dynamic_slice(expert_up[0], (dp * 32, 0), (32, 512))
    down_part = lax.dynamic_slice(expert_down[0], (dp % 16 * 16, dp // 16 * 512), (16, 512))
    part = jnp.concatenate([up_part, down_part], axis=0)
    column = lax.all_gather(part, "seq", axis=0).reshape(CHIPS, 2, 48, 512)
    column = lax.dynamic_index_in_dim(column, core, 1, keepdims=False)
    whole = lax.all_gather(column, "dp", axis=0)
    proj = lax.all_gather(out_weight, "seq", axis=0, tiled=True)
    gates = jnp.sum(
        jnp.where(expert_ids[:, :, None] == jnp.arange(16), gate_weights[:, :, None], 0.0), axis=1
    )
    sib_gates = lax.ppermute(gates, "seq", [(i, i ^ 1) for i in range(16)])
    ctx = attend(keyvals.transpose(1, 0, 2), queries)
    return experts(
        ctx, residual, proj, norm_gain[None], gates, sib_gates, whole[:, :, :32], whole[:, :, 32:]
    )


def solution(mesh):
    rows = P(("dp", "seq"), None)
    placed = (
        rows,
        P(("dp", "seq"), None, None),
        rows,
        P("seq", None),
        P(),
        P("seq", None, None),
        P("seq", None, None),
        rows,
        rows,
        rows,
    )
    return jax.shard_map(body, mesh=mesh, in_specs=placed, out_specs=rows, check_vma=False)
```

time: 526 us -> 223 us (0.42); the launches traced: 518 us -> 222 us
  matrix products: 185 us -> 0 us
  waiting for transfers between devices: 177 us -> 58.8 us
  Pallas kernels: 0 us -> 101 us
  blocking collectives: 65 us -> 23.5 us
  other arithmetic: 25.7 us -> 0.73 us
  starting transfers between devices: 24.7 us -> 2.11 us
    dot_general x156 -> x0, matrix products: 185 us -> none  [the longest x76 89.9 us: key_step(): jnp.einsum('qhd,khd->hqk', tile_query, tile_keys[..., :head_size], prefer...]
    all_to_all x4 -> x0, waiting for transfers between devices: 177 us -> none  [the longest x1 102 us: body(): lax.all_to_all(repeated, 'seq', split_axis=1, concat_axis=0, tiled=True)]
    pallas_call x0 -> x2, Pallas kernels: none -> 101 us  [the longest x1 89.1 us: attend(): pl.pallas_call(attend_kernel, out_shape=jax.ShapeDtypeStruct((ROWS, 1024)...]
    all_to_all x1 -> x0, blocking collectives: 65 us -> none  [body(): lax.all_to_all(outgoing, 'seq', split_axis=0, concat_axis=1, tiled=True)]
    all_gather x1 -> x2, waiting for transfers between devices: 0.02 us -> 58.8 us  [the longest x1 30.6 us: body(): whole = lax.all_gather(column, 'dp', axis=0)]
    all_to_all x4 -> x0, starting transfers between devices: 24.7 us -> none  [the longest x1 10.2 us: body(): lax.all_to_all(queries, 'seq', split_axis=1, concat_axis=0, tiled=True)]
    all_gather x0 -> x1, blocking collectives: none -> 23.5 us  [body(): column = lax.all_gather(part, 'seq', axis=0).reshape(CHIPS, 2, 48, 512)]
    reduce_sum x77 -> x1, other arithmetic: 15.1 us -> 0.72 us  [body(): jnp.sum(jnp.where(expert_ids[:, :, None] == jnp.arange(16), gate_weights[...]
  transfers between devices with their start and end apart: 5 -> 3, of which waited for: 4 -> 2; matrix products, arithmetic and copies ran while one was open for 41% -> 7% of each run, Pallas kernels for 0% -> 40%
where the time goes in v1:
time: 223 us; the launch traced here: 222 us
  Pallas kernels  101 us (45%)
  waiting for transfers between devices  58.8 us (26%)
  blocking collectives  23.5 us (11%)
  local copies, waits for them, and re-layouts  22.4 us (10%)
  between operations  13.4 us (6%)
    pallas_call x1, Pallas kernels, attend(): pl.pallas_call(attend_kernel, out_shape=jax.ShapeDtypeStruct((ROWS, 1024)...  89.1 us
    all_gather x1, waiting for transfers between devices, body(): whole = lax.all_gather(column, 'dp', axis=0)  30.6 us
    all_gather x1, waiting for transfers between devices, body(): proj = lax.all_gather(out_weight, 'seq', axis=0, tiled=True)  28.2 us
    all_gather x1, blocking collectives, body(): column = lax.all_gather(part, 'seq', axis=0).reshape(CHIPS, 2, 48, 512)  23.5 us
    pallas_call x1, Pallas kernels, experts(): pl.pallas_call(experts_kernel, out_shape=jax.ShapeDtypeStruct((ROWS, 1024...  12 us
    slice x1, local copies, waits for them, and re-layouts, body(): whole[:, :, :32]  8.28 us
    unnamed x14, local copies, waits for them, and re-layouts  7.58 us
    slice x1, local copies, waits for them, and re-layouts, body(): whole[:, :, 32:]  4.95 us
  transfers between devices with their start and end apart: 3, of which 2 were waited for; matrix products, arithmetic and copies ran while one was open for 7% of the time, Pallas kernels for 40%

profile of v1, /device:TPU:1, one launch (start us, length us, event | category | flops | bytes accessed | tf_op | source)
XLA Modules:
  0.0 222.1 jit_solution(9922665910341873704)
XLA Ops:
  6.5 0.0 copy-start
  6.5 0.0 copy-start.5
  6.5 0.0 all-gather.7.cloned.1.call-start
  6.5 1.2 copy-done
  7.8 0.7 dynamic-slice_bitcast_fusion.1
  8.5 23.5 %all-gather = bf16[768,512]{1,0:T(8,128)(2,1)S(1)} all-gather(bf16[48,512]{1,0:T(8,128)(2,1)S(1)} %pad_maximum_fusion), channel_id=2, replica_groups=mesh['dp'=32,'seq'=16] {'seq'}, dimensions={0}, use_global_device_ids=true | all-gather | bytes 835584 | tf_op jit(solution)/shard_map/all_gather | solution.py:265
  32.0 0.8 constant_dynamic-slice_fusion
  32.8 0.0 all-gather.7.cloned.1.call-update
  32.8 0.0 all-gather.5.cloned.1.call-start
  32.9 0.7 select_reduce_fusion
  33.6 0.1 copy.21.gates
  33.7 2.1 collective-permute-start
  35.8 0.0 all-gather.5.cloned.1.call-update
  35.8 1.9 copy.23
  37.7 0.0 copy-done.5
  37.7 89.1 %shard_map.91.ctx = bf16[128,1024]{1,0:T(8,128)(2,1)S(1)} custom-call(bf16[8,1024,128]{2,1,0:T(8,128)(2,1)S(1)} %bitcast.10, bf16[128,1024]{1,0:T(8,128)(2,1)S(1)} %copy-done.5), custom_call_target="tpu_custom_call" | custom-call | flops 60000002048 | bytes 100000000 | tf_op jit(solution)/shard_map/pallas_call | solution.py:171
  126.8 30.6 %all-gather.7.cloned.1.call-done = bf16[256,1,48,512]{3,2,1,0:T(8,128)(2,1)} async-done(((bf16[8,1,48,512]{3,2,1,0:T(8,128)(2,1)}), bf16[256,1,48,512]{3,2,1,0:T(8,128)(2,1)}) %all-gather.7.cloned.1.call-update) | async-done | bytes 12582928 | tf_op jit(solution)/shard_map/all_gather | solution.py:267
  157.4 8.3 %slice.8.up = bf16[32,8,32,512]{3,2,1,0:T(8,128)(2,1)} slice(bf16[32,8,48,512]{3,2,1,0:T(8,128)(2,1)} %bitcast.12), slice={[0:32], [0:8], [0:32], [0:512]} | slice | bytes 16777216 | tf_op jit(solution)/shard_map/slice | solution.py:275
  165.7 0.0 copy-start.3
  165.7 0.0 copy-start.4
  165.7 4.9 %slice.9.down = bf16[32,8,16,512]{3,2,1,0:T(8,128)(2,1)} slice(bf16[32,8,48,512]{3,2,1,0:T(8,128)(2,1)} %bitcast.13), slice={[0:32], [0:8], [32:48], [0:512]} | slice | bytes 8388608 | tf_op jit(solution)/shard_map/slice | solution.py:275
  170.6 0.0 collective-permute-done.sib_gates
  170.6 28.2 %all-gather.5.cloned.1.call-done.proj = bf16[1024,1024]{1,0:T(8,128)(2,1)} async-done(((bf16[64,1024]{1,0:T(8,128)(2,1)}), bf16[1024,1024]{1,0:T(8,128)(2,1)}) %all-gather.5.cloned.1.call-update) | async-done | bytes 2097168 | tf_op jit(solution)/shard_map/all_gather | solution.py:268
  198.8 0.0 copy-done.3
  198.8 0.0 copy-done.4
  198.8 0.0 copy-start.1
  198.8 2.2 copy-done.1
  201.0 0.0 copy-start.2
  201.0 1.6 copy-done.2
  202.6 12.0 %shard_map.92 = bf16[128,1024]{1,0:T(8,128)(2,1)S(1)} custom-call(bf16[128,1024]{1,0:T(8,128)(2,1)S(1)} %shard_map.91.ctx, bf16[128,1024]{1,0:T(8,128)(2,1)S(1)} %copy-done.3, bf16[1024,1024]{1,0:T(8,128)(2,1)S(1)} %copy-done.2, f32[1,1024]{1,0:T(1,128)S(1)} %bitcast.11, f32[128,16]{1,0:T(8,128)S(1)} %copy.21.gates, ...), custom_call_target="tpu_custom_call" | custom-call | tf_op jit(solution)/shard_map/pallas_call | solution.py:240
  214.6 0.7 copy.25
  (2 shorter events, 0.0 us)
Async XLA Ops:
  6.5 1.2 copy-start
  6.5 31.1 %copy-start.5 = (bf16[128,1024]{1,0:T(8,128)(2,1)S(1)}, bf16[128,1024]{1,0:T(8,128)(2,1)}, u32[]{:S(2)}) copy-start(bf16[128,1024]{1,0:T(8,128)(2,1)} %q.1) | copy-start | bytes 786436
  6.5 150.9 %all-gather.7.cloned.1.call-start = ((), (), s32[]{:S(2)}) async-start(), calls=%async_computation.1 | async-start | bytes 12976128 | tf_op jit(solution)/shard_map/all_gather | solution.py:267
  32.8 166.0 %all-gather.5.cloned.1.call-start = ((), (), s32[]{:S(2)}) async-start(), calls=%async_computation | async-start | bytes 2228224 | tf_op jit(solution)/shard_map/all_gather | solution.py:268
  33.7 136.9 %collective-permute-start = (f32[128,16]{1,0:T(8,128)S(1)}, f32[128,16]{1,0:T(8,128)S(1)}, u32[]{:S(2)}, u32[]{:S(2)}) collective-permute-start(f32[128,16]{1,0:T(8,128)S(1)} %copy.21.gates), channel_id=1, source_target_pairs={{0,1},{1,0},{2,3},{3,2},{4,5},{5,4},{6,7},{7,6},{8,9},{9,8},{10,11... | collective-permute-start | bytes 24584 | tf_op jit(solution)/shard_map/ppermute | solution.py:272
  165.7 33.1 %copy-start.3 = (bf16[128,1024]{1,0:T(8,128)(2,1)S(1)}, bf16[128,1024]{1,0:T(8,128)(2,1)}, u32[]{:S(2)}) copy-start(bf16[128,1024]{1,0:T(8,128)(2,1)} %residual.1) | copy-start | bytes 786436
  165.7 33.1 %copy-start.4 = (f32[1024]{0:T(1024)S(1)}, f32[1024]{0:T(1024)}, u32[]{:S(2)}) copy-start(f32[1024]{0:T(1024)} %param.14) | copy-start | bytes 12292
  198.8 2.2 copy-start.1
  201.0 1.6 copy-start.2
Sparse Core Ops, SparseCore 0:
  33.0 124.3 all-gather.6
  159.5 39.2 all-gather.4

commit v2 on v0

v2 whole, which is shorter than its diff:
```python
import jax
import jax.numpy as jnp
from jax import lax
from jax.experimental import pallas as pl
from jax.experimental.pallas import tpu as pltpu
from jax.sharding import PartitionSpec as P

CHIPS = 8
XS = 4
ZS = 8
ROWS = 128
KEYS = 1024
HEAD = 64
FF = 256
SLOTS = 10
LOW = -1e30
MESH = pl.DeviceIdType.MESH
OFFSETS = (1, 7, 2, 6, 3, 5, 4)
TRANSFERS = 128


def chip_columns(chip):
    return pl.ds(pl.multiple_of(chip * 128, 128), 128)


def rows_at(start, size):
    return pl.ds(pl.multiple_of(start, size), size)


def layer_kernel(
    kv, q, residual, proj, gain, own_up, own_down, ids, chosen, out,
    kvland, qland, qt, vt, acc, top, sa, sb, pa, pb, aa, ab, mland, cbuf, cland,
    ups, downs, weight, gates, x, hid, total, yland, own_sem, snd, rcv,
):
    f32, bf16 = jnp.float32, jnp.bfloat16
    s = lax.axis_index("seq")
    c = s // 2
    k = lax.rem(s, 2)
    sib = s + 1 - 2 * k
    dp = lax.axis_index("dp")
    px = dp // ZS
    pz = lax.rem(dp, ZS)

    def chip(d):
        return lax.rem(c + d + CHIPS, CHIPS)

    def peer(d):
        return chip(d) * 2 + k

    def xat(i):
        return lax.rem(px + i + XS, XS)

    def zat(i):
        return lax.rem(pz + i + ZS, ZS)

    def plane(i, j):
        return xat(i) * ZS + zat(j)

    sent = []

    def transfer(src, dst, **where):
        n = len(sent)
        copy = pltpu.make_async_remote_copy(
            src_ref=src, dst_ref=dst, send_sem=snd.at[n], recv_sem=rcv.at[n], device_id=where, device_id_type=MESH
        )
        sent.append(copy)
        return copy

    def begin(*copies):
        for copy in copies:
            copy.start()

    def arrive(*copies):
        for copy in copies:
            copy.wait_recv()

    barrier = pltpu.get_barrier_semaphore()
    others = [{"seq": peer(d)} for d in OFFSETS] + [{"seq": sib}]
    others += [{"dp": plane(i, 0)} for i in (1, 2, 3)] + [{"dp": plane(0, j)} for j in (1, -1)]
    for where in others:
        pl.semaphore_signal(barrier, inc=1, device_id=where, device_id_type=MESH)
    own_kv = pltpu.make_async_copy(kv.at[c], kvland.at[0], own_sem)
    own_kv.start()
    qland[s] = q[:, chip_columns(c)]
    lane = lax.broadcasted_iota(jnp.int32, (ROWS, 128), 1)
    mine = jnp.zeros((ROWS, 128), f32)
    for j in range(ids.shape[1]):
        mine = mine + jnp.where(lane == ids[:, j : j + 1], chosen[:, j : j + 1], 0.0)
    gates[0:ROWS, :] = mine
    downs[pz, px, 7 + c // 4, :, chip_columns(lax.rem(c, 4))] = proj[rows_at(px * 16, 16), chip_columns(pz)]
    pl.semaphore_wait(barrier, len(others))

    quarter = pz * XS + px
    first = []
    for d in OFFSETS:
        slot = CHIPS - d - 1
        first.append(transfer(own_up.at[0, rows_at(dp * 32, 32)], ups.at[dp, slot], seq=peer(d)))
        first.append(
            transfer(
                own_down.at[0, rows_at(lax.rem(quarter, 16) * 16, 16), pl.ds(pl.multiple_of(quarter // 16 * 512, 512), 512)],
                downs.at[pz, px, slot],
                seq=peer(d),
            )
        )
        first.append(
            transfer(
                proj.at[rows_at(px * 16, 16), chip_columns(pz)],
                downs.at[pz, px, 7 + c // 4, :, chip_columns(lax.rem(c, 4))],
                seq=peer(d),
            )
        )
    begin(*first)

    q_out = {d: transfer(q.at[:, chip_columns(chip(d))], qland.at[s], seq=peer(d)) for d in OFFSETS}
    kv_out = {d: transfer(kv.at[chip(d)], kvland.at[d], seq=peer(d)) for d in OFFSETS}
    q_on = {d: transfer(qland.at[peer(-d)], qland.at[peer(-d)], seq=sib) for d in (0,) + OFFSETS}
    gate_on = transfer(gates.at[pl.ds(0, ROWS)], gates.at[pl.ds(ROWS, ROWS)], seq=sib)
    begin(*q_out.values())
    begin(q_on[0], gate_on)
    begin(*kv_out.values())

    def up_to(i, j, **where):
        return transfer(ups.at[plane(i, j)], ups.at[plane(i, j)], **where)

    def down_to(j, part=None, **where):
        ref = downs.at[zat(j)] if part is None else downs.at[zat(j), pl.ds(part, 2)]
        return transfer(ref, ref, **where)

    right, left = {"dp": plane(1, 0)}, {"dp": plane(-1, 0)}
    upward, downward = {"dp": plane(0, 1)}, {"dp": plane(0, -1)}
    zp = {i: up_to(0, 1 - i, **upward) for i in (1, 2, 3, 4)}
    zm = {i: up_to(0, i - 1, **downward) for i in (1, 2, 3)}
    around = (0, 1, -1, 2, -2, 3, -3, 4)
    xp = {o: up_to(0, o, **right) for o in around}
    xm = {o: up_to(0, o, **left) for o in around}
    xf = {o: up_to(-1, o, **right) for o in (0, 1, 2, 3)}
    xf.update({o: up_to(1, o, **left) for o in (-1, -2, -3, 4)})
    bx = [transfer(downs.at[pz, px], downs.at[pz, px], dp=plane(i, 0)) for i in (1, -1, 2)]
    bp = {i: down_to(1 - i, **upward) for i in (1, 2, 3)}
    bm = {i: down_to(i - 1, **downward) for i in (1, 2, 3)}
    bp[4] = down_to(-3, 0, **upward)
    bm[4] = down_to(3, 2, **downward)

    def w1():
        arrive(*first)
        begin(zp[1], zm[1], xp[0], xm[0], *bx)

    def w2():
        arrive(zp[1], zm[1])
        begin(zp[2], zm[2], xp[-1], xm[-1], xp[1], xm[1])

    def w3():
        arrive(*bx)
        begin(bp[1], bm[1])

    def w4():
        arrive(zp[2], zm[2])
        begin(zp[3], zm[3], xp[-2], xm[-2], xp[2], xm[2])

    def w5():
        arrive(xp[0])
        begin(xf[0])

    def w6():
        arrive(zp[3], zm[3])
        begin(zp[4], xp[-3], xm[-3], xp[3], xm[3])

    def w7():
        arrive(bp[1], bm[1])
        begin(bp[2], bm[2])

    def w8():
        arrive(zp[4])
        begin(xp[4], xm[4])

    def w9():
        arrive(xp[1], xm[-1])
        begin(xf[1], xf[-1])

    def w10():
        arrive(bp[2], bm[2])
        begin(bp[3], bm[3])

    def w11():
        arrive(xp[2], xm[-2])
        begin(xf[2], xf[-2])

    def w12():
        arrive(xp[3], xm[-3])
        begin(xf[3], xf[-3])

    def w13():
        arrive(bp[3], bm[3])
        begin(bp[4], bm[4])

    def w14():
        arrive(xm[4])
        begin(xf[4])

    def w15():
        arrive(xm[0], xm[1], xp[-1], xm[2], xp[-2], xm[3], xp[-3], xp[4])
        arrive(*xf.values())
        arrive(bp[4], bm[4])

    acc[...] = jnp.zeros_like(acc)
    top[...] = jnp.full_like(top, LOW)
    vt[HEAD:, :] = jnp.ones((16, KEYS), bf16)
    qt[...] = jnp.zeros_like(qt)

    for d in OFFSETS:
        arrive(q_out[d])
        begin(q_on[d])
    w1()
    arrive(*q_on.values())

    def prepare(t, carry):
        y = jnp.transpose(qland[t].astype(f32) * (HEAD**-0.5)).astype(bf16)
        qt[t, 0:HEAD, 0:ROWS] = y[0:HEAD]
        qt[t, 0:HEAD, ROWS:] = y[HEAD:]
        return carry

    lax.fori_loop(0, 2 * CHIPS, prepare, 0)

    def place(t):
        return lax.rem(t, 2) * SLOTS + t // 2

    def process(d):
        source = peer(-d)
        for r in range(0, KEYS, 128):
            block = jnp.transpose(kvland[d, r : r + 128, :].astype(f32))
            vt[0:HEAD, r : r + 128] = block[HEAD:, :].astype(bf16)

        scores = jnp.dot(kvland[d, 0:ROWS, :], qt[source], preferred_element_type=f32)
        key_row = lax.broadcasted_iota(jnp.int32, (ROWS, 2 * ROWS), 0)
        query_row = lax.rem(lax.broadcasted_iota(jnp.int32, (ROWS, 2 * ROWS), 1), ROWS)
        scores = jnp.where(key_row <= query_row, scores, LOW)
        i = place(source)
        old = top[i]
        new = jnp.maximum(old, jnp.max(scores, axis=0, keepdims=True))
        probs = jnp.where(key_row <= query_row, jnp.exp(scores - new), 0.0).astype(bf16)
        acc[i] = acc[i] * jnp.exp(old - new) + jnp.dot(vt[:, 0:ROWS], probs, preferred_element_type=f32)
        top[i] = new

        def score(n, scores):
            scores[...] = jnp.dot(kvland[d], qt[source + 1 + n], preferred_element_type=f32)

        def soften(n, scores, probs, shrink):
            i = place(source + 1 + n)
            old = top[i]
            new = jnp.maximum(old, jnp.max(scores[...], axis=0, keepdims=True))
            probs[...] = jnp.exp(scores[...] - new).astype(bf16)
            shrink[...] = jnp.exp(old - new)
            top[i] = new

        def add(n, probs, shrink):
            i = place(source + 1 + n)
            acc[i] = acc[i] * shrink[...] + jnp.dot(vt[...], probs[...], preferred_element_type=f32)

        score(0, sa)
        soften(0, sa, pa, aa)
        score(1, sb)

        def step(m, carry):
            n = 2 * m
            score(n + 2, sa)
            soften(n + 1, sb, pb, ab)
            add(n, pa, aa)
            score(n + 3, sb)
            soften(n + 2, sa, pa, aa)
            add(n + 1, pb, ab)
            return carry

        lax.fori_loop(0, (2 * CHIPS - source) // 2, step, 0)

    own_kv.wait()
    process(0)
    for d, services in zip(
        OFFSETS, ((w2, w3, w5), (w4,), (w6, w7), (w8, w9), (w10, w11), (w12,), (w13, w14))
    ):
        for service in services:
            service()
        arrive(kv_out[d])
        process(d)

    def note(i, carry):
        acc[i, 72:80, :] = jnp.broadcast_to(top[i], (8, 2 * ROWS))
        return carry

    lax.fori_loop(0, 2 * SLOTS, note, 0)
    swap = transfer(acc.at[pl.ds((1 - k) * SLOTS, CHIPS)], mland, seq=sib)
    begin(swap)
    arrive(swap)

    def finish(i):
        mine, theirs = acc[k * SLOTS + i], mland[i]
        ma, mb = mine[72:73], theirs[72:73]
        both = jnp.maximum(ma, mb)
        merged = mine * jnp.exp(ma - both) + theirs * jnp.exp(mb - both)
        ctx = merged[0:HEAD] / merged[HEAD : HEAD + 1]
        ctx = jnp.concatenate([ctx[:, 0:ROWS], ctx[:, ROWS:]], axis=0)
        return jnp.transpose(ctx).astype(bf16)

    c_out = {d: transfer(cbuf.at[d], cland.at[:, chip_columns(c)], seq=peer(d)) for d in OFFSETS}
    for d in OFFSETS:
        cbuf[d] = finish(chip(d))
        begin(c_out[d])
    cland[:, chip_columns(c)] = finish(c)
    w15()

    for i in range(CHIPS):
        for j in range(ZS):
            block = downs[j, :, 7 + i // 4, :, 128 * (i % 4) : 128 * (i % 4) + 128]
            weight[i, k, :, 128 * j : 128 * j + 128] = block.reshape(HEAD, 128)
    w_on = transfer(weight.at[:, k], weight.at[:, k], seq=sib)
    begin(w_on)
    arrive(w_on)
    arrive(*c_out.values())

    hidden = (
        residual[...].astype(f32)
        + jnp.dot(cland[...], weight[...].reshape(1024, 1024), preferred_element_type=f32)
    ).astype(bf16)
    hid[...] = hidden
    wide = hidden.astype(f32)
    normed = wide * lax.rsqrt(jnp.mean(wide * wide, axis=-1, keepdims=True) + 1e-05) * gain[...]
    x[0:ROWS, :] = normed.astype(bf16)
    x_on = transfer(x.at[pl.ds(0, ROWS)], x.at[pl.ds(ROWS, ROWS)], seq=sib)
    begin(x_on)
    arrive(x_on, gate_on)

    def expert(e, up, low, high):
        projected = jnp.dot(x[...], up, preferred_element_type=f32)
        gate, lift = projected[:, :FF], projected[:, FF:]
        column = lax.broadcasted_iota(jnp.int32, (2 * ROWS, 128), 1)
        scale = jnp.sum(jnp.where(column == e, gates[...], 0.0), axis=1, keepdims=True)
        act = (gate / (1.0 + jnp.exp(-gate)) * lift * scale).astype(bf16)
        return (
            jnp.dot(act, low, preferred_element_type=f32),
            jnp.dot(act, high, preferred_element_type=f32),
        )

    low, high = expert(s, own_up[0], own_down[0, :, 0:512], own_down[0, :, 512:])
    total[:, 0:512] = low
    total[:, 512:] = high

    def other(j, carry):
        low, high = expert(
            chip(j + 1) * 2 + k,
            ups[:, j].reshape(1024, 512),
            downs[0:4, :, j].reshape(FF, 512),
            downs[4:8, :, j].reshape(FF, 512),
        )
        total[:, 0:512] += low
        total[:, 512:] += high
        return carry

    lax.fori_loop(0, CHIPS - 1, other, 0)
    y_on = transfer(total.at[pl.ds(ROWS, ROWS)], yland, seq=sib)
    begin(y_on)
    arrive(y_on)
    out[...] = (hid[...].astype(f32) + total[0:ROWS, :] + yland[...]).astype(bf16)
    for copy in sent:
        copy.wait_send()


def body(
    queries, keyvals, residual, out_weight, norm_gain, expert_up, expert_down, expert_ids, slot_index, gate_weights
):
    dma = pltpu.SemaphoreType.DMA
    vmem = pl.BlockSpec(memory_space=pltpu.VMEM)
    f32, bf16 = jnp.float32, jnp.bfloat16
    return pl.pallas_call(
        layer_kernel,
        out_shape=jax.ShapeDtypeStruct((ROWS, 1024), bf16),
        in_specs=[vmem] * 9,
        out_specs=vmem,
        scratch_shapes=[
            pltpu.VMEM((CHIPS, KEYS, 128), bf16),
            pltpu.VMEM((2 * CHIPS, ROWS, 128), bf16),
            pltpu.VMEM((2 * SLOTS, 128, 2 * ROWS), bf16),
            pltpu.VMEM((HEAD + 16, KEYS), bf16),
            pltpu.VMEM((2 * SLOTS, HEAD + 16, 2 * ROWS), f32),
            pltpu.VMEM((2 * SLOTS, 1, 2 * ROWS), f32),
            pltpu.VMEM((KEYS, 2 * ROWS), f32),
            pltpu.VMEM((KEYS, 2 * ROWS), f32),
            pltpu.VMEM((KEYS, 2 * ROWS), bf16),
            pltpu.VMEM((KEYS, 2 * ROWS), bf16),
            pltpu.VMEM((1, 2 * ROWS), f32),
            pltpu.VMEM((1, 2 * ROWS), f32),
            pltpu.VMEM((CHIPS, HEAD + 16, 2 * ROWS), f32),
            pltpu.VMEM((CHIPS, ROWS, 128), bf16),
            pltpu.VMEM((ROWS, 1024), bf16),
            pltpu.VMEM((XS * ZS, CHIPS - 1, 32, 512), bf16),
            pltpu.VMEM((ZS, XS, CHIPS + 1, 16, 512), bf16),
            pltpu.VMEM((CHIPS, 2, HEAD, 1024), bf16),
            pltpu.VMEM((2 * ROWS, 128), f32),
            pltpu.VMEM((2 * ROWS, 1024), bf16),
            pltpu.VMEM((ROWS, 1024), bf16),
            pltpu.VMEM((2 * ROWS, 1024), f32),
            pltpu.VMEM((ROWS, 1024), f32),
            dma,
            dma((TRANSFERS,)),
            dma((TRANSFERS,)),
        ],
        compiler_params=pltpu.CompilerParams(
            collective_id=0, has_side_effects=True, vmem_limit_bytes=56 * 1024 * 1024
        ),
        cost_estimate=pl.CostEstimate(flops=60_000_000_000, bytes_accessed=100_000_000, transcendentals=16_000_000),
    )(
        keyvals.transpose(1, 0, 2), queries, residual, out_weight, norm_gain[None], expert_up, expert_down,
        expert_ids, gate_weights,
    )


def solution(mesh):
    rows = P(("dp", "seq"), None)
    placed = (
        rows,
        P(("dp", "seq"), None, None),
        rows,
        P("seq", None),
        P(),
        P("seq", None, None),
        P("seq", None, None),
        rows,
        rows,
        rows,
    )
    return jax.shard_map(body, mesh=mesh, in_specs=placed, out_specs=rows, check_vma=False)
```

time: 526 us -> 134 us (0.25); the launches traced: 518 us -> 134 us
  matrix products: 185 us -> 0 us
  waiting for transfers between devices: 177 us -> 0 us
  Pallas kernels: 0 us -> 126 us
  blocking collectives: 65 us -> 0 us
  other arithmetic: 25.7 us -> 0 us
  starting transfers between devices: 24.7 us -> 0 us
  local copies, waits for them, and re-layouts: 22 us -> 7.7 us
  between operations: 13.6 us -> 0.01 us
    dot_general x156 -> x0, matrix products: 185 us -> none  [the longest x76 89.9 us: key_step(): jnp.einsum('qhd,khd->hqk', tile_query, tile_keys[..., :head_size], prefer...]
    all_to_all x4 -> x0, waiting for transfers between devices: 177 us -> none  [the longest x1 102 us: body(): lax.all_to_all(repeated, 'seq', split_axis=1, concat_axis=0, tiled=True)]
    pallas_call x0 -> x1, Pallas kernels: none -> 126 us  [body(): pl.pallas_call(layer_kernel, out_shape=jax.ShapeDtypeStruct((ROWS, 1024),...]
    all_to_all x1 -> x0, blocking collectives: 65 us -> none  [body(): lax.all_to_all(outgoing, 'seq', split_axis=0, concat_axis=1, tiled=True)]
    all_to_all x4 -> x0, starting transfers between devices: 24.7 us -> none  [the longest x1 10.2 us: body(): lax.all_to_all(queries, 'seq', split_axis=1, concat_axis=0, tiled=True)]
    reduce_sum x77 -> x0, other arithmetic: 15.1 us -> none  [the longest x76 15 us: key_step(): totals = totals * shrink + jnp.sum(weights, axis=-1)]
    gather x1 -> x0, local copies, waits for them, and re-layouts: 7.05 us -> none  [body(): picked = jnp.take(flat_back, target, axis=0)]
    while x77 -> x0, local copies, waits for them, and re-layouts: 6.62 us -> none  [the longest x1 6.42 us: attend(): return lax.fori_loop(0, query_count // query_tile, query_step, blank_out)]
  transfers between devices with their start and end apart: 5 -> 0, of which waited for: 4 -> 0; matrix products, arithmetic and copies ran while one was open for 41% -> 0% of each run, Pallas kernels for 0% -> 0%
where the time goes in v2:
time: 134 us
  Pallas kernels  126 us (94%)
  local copies, waits for them, and re-layouts  7.7 us (6%)
    pallas_call x1, Pallas kernels, body(): pl.pallas_call(layer_kernel, out_shape=jax.ShapeDtypeStruct((ROWS, 1024),...  126 us
    unnamed x4, local copies, waits for them, and re-layouts  7.7 us

profile of v2, /device:TPU:1, one launch (start us, length us, event | category | flops | bytes accessed | tf_op | source)
XLA Modules:
  0.0 133.8 jit_solution(17113704661027458539)
XLA Ops:
  0.0 1.4 %copy.11.ids = s32[128,8]{1,0:T(8,128)} copy(s32[128,8]{0,1:T(8,128)} %param.17) | data formatting | bytes 8192 | tf_op args[7]
  1.4 1.4 %copy.12.chosen = f32[128,8]{1,0:T(8,128)} copy(f32[128,8]{0,1:T(8,128)} %param.18) | data formatting | bytes 8192 | tf_op args[9]
  2.8 3.2 %copy.14 = bf16[1024,8,128]{2,0,1:T(8,128)(2,1)} copy(bf16[1024,8,128]{2,1,0:T(8,128)(2,1)} %param.11) | data formatting | bytes 4194304 | tf_op args[1]
  6.0 126.1 %shard_map.91 = bf16[128,1024]{1,0:T(8,128)(2,1)} custom-call(bf16[8,1024,128]{2,1,0:T(8,128)(2,1)} %bitcast.4, bf16[128,1024]{1,0:T(8,128)(2,1)} %q.1, bf16[128,1024]{1,0:T(8,128)(2,1)} %residual.1, bf16[64,1024]{1,0:T(8,128)(2,1)} %proj.1, f32[1,1024]{1,0:T(1,128)} %bitcast.5, bf16[1,1024,512]{2,1,0:T(8,128)(2,1)} %own_up.1, ...), custom_call_target="tpu_custom_call" | custom-call | flops 60000002048 | bytes 100000000 | tf_op jit(solution)/shard_map/pallas_call | solution.py:372
  132.1 1.7 %copy.16 = bf16[128,1024]{1,0:T(8,128)(2,1)} copy(bf16[128,1024]{1,0:T(8,128)(2,1)} %shard_map.91) | data formatting | bytes 524288

commit v3 on v2

v3 whole, which is shorter than its diff:
```python
import jax
import jax.numpy as jnp
from jax import lax
from jax.experimental import pallas as pl
from jax.experimental.pallas import tpu as pltpu
from jax.sharding import PartitionSpec as P

CHIPS = 8
XS = 4
ZS = 8
ROWS = 128
KEYS = 1024
HEAD = 64
FF = 256
LOW = -1e30
MESH = pl.DeviceIdType.MESH
OFFSETS = (1, 7, 2, 6, 3, 5, 4)
TRANSFERS = 128


def chip_columns(chip):
    return pl.ds(pl.multiple_of(chip * 128, 128), 128)


def rows_at(start, size):
    return pl.ds(pl.multiple_of(start, size), size)


def layer_kernel(
    kv, q, residual, proj, gain, up_in, down_in, ids, chosen, out,
    kvland, qland, qt, vt, acc, top, sa, sb, pa, pb, aa, ab, cbuf, cland,
    own_up, own_down, ups, downs, projs, weight, gates, x, hid, total, yland, own_sem, up_sem, down_sem, snd, rcv,
):
    f32, bf16 = jnp.float32, jnp.bfloat16
    s = lax.axis_index("seq")
    c = s // 2
    k = lax.rem(s, 2)
    sib = s + 1 - 2 * k
    dp = lax.axis_index("dp")
    px = dp // ZS
    pz = lax.rem(dp, ZS)

    def chip(d):
        return lax.rem(c + d + CHIPS, CHIPS)

    def peer(d):
        return chip(d) * 2 + k

    def xat(i):
        return lax.rem(px + i + XS, XS)

    def zat(i):
        return lax.rem(pz + i + ZS, ZS)

    def plane(i, j):
        return xat(i) * ZS + zat(j)

    sent = []

    def transfer(src, dst, **where):
        n = len(sent)
        copy = pltpu.make_async_remote_copy(
            src_ref=src, dst_ref=dst, send_sem=snd.at[n], recv_sem=rcv.at[n], device_id=where, device_id_type=MESH
        )
        sent.append(copy)
        return copy

    def begin(*copies):
        for copy in copies:
            copy.start()

    def arrive(*copies):
        for copy in copies:
            copy.wait_recv()

    barrier = pltpu.get_barrier_semaphore()
    others = [{"seq": peer(d)} for d in OFFSETS] + [{"seq": sib}]
    others += [{"dp": plane(i, 0)} for i in (1, 2, 3)] + [{"dp": plane(0, j)} for j in (1, -1)]
    for where in others:
        pl.semaphore_signal(barrier, inc=1, device_id=where, device_id_type=MESH)
    own_kv = pltpu.make_async_copy(kv.at[c], kvland.at[0, 0], own_sem)
    own_kv.start()
    up_copy = pltpu.make_async_copy(up_in.at[0], own_up, up_sem)
    up_copy.start()
    down_copy = pltpu.make_async_copy(down_in.at[0], own_down, down_sem)
    down_copy.start()
    qland[c] = q[:, chip_columns(c)]
    expert_row = lax.broadcasted_iota(jnp.int32, (128, ROWS), 0)
    mine = jnp.zeros((128, ROWS), f32)
    for j in range(ids.shape[0]):
        mine = mine + jnp.where(expert_row == ids[j : j + 1, :], chosen[j : j + 1, :], 0.0)
    gates[0:ROWS, :] = jnp.transpose(mine)
    projs[pz, px, c // 4, :, chip_columns(lax.rem(c, 4))] = proj[rows_at(px * 16, 16), chip_columns(pz)]
    pl.semaphore_wait(barrier, len(others))

    quarter = pz * XS + px
    first = [
        transfer(up_in.at[0, rows_at(dp * 32, 32)], ups.at[dp, CHIPS - d - 1], seq=peer(d)) for d in OFFSETS
    ]
    second = []
    for d in OFFSETS:
        second.append(
            transfer(
                proj.at[rows_at(px * 16, 16), chip_columns(pz)],
                projs.at[pz, px, c // 4, :, chip_columns(lax.rem(c, 4))],
                seq=peer(d),
            )
        )
        part = pl.ds(pl.multiple_of(quarter // 16 * 512, 512), 512)
        second.append(
            transfer(
                down_in.at[0, rows_at(lax.rem(quarter, 16) * 16, 16), part],
                downs.at[pz, px, CHIPS - d - 1],
                seq=peer(d),
            )
        )
    begin(*first, *second)

    q_out = {d: transfer(q.at[:, chip_columns(chip(d))], qland.at[c], seq=peer(d)) for d in OFFSETS}
    kv_out = {d: transfer(kv.at[chip(d)], kvland.at[0, d], seq=peer(d)) for d in OFFSETS}
    kv_on = {d: transfer(kvland.at[0, d], kvland.at[1, d], seq=sib) for d in (0,) + OFFSETS}
    gate_on = transfer(gates.at[pl.ds(0, ROWS)], gates.at[pl.ds(ROWS, ROWS)], seq=sib)
    begin(*q_out.values())
    begin(*[kv_out[d] for d in OFFSETS[:4]])
    own_kv.wait()
    begin(kv_on[0], gate_on)

    def up_to(i, j, **where):
        return transfer(ups.at[plane(i, j)], ups.at[plane(i, j)], **where)

    def row_to(rows, j, part=None, **where):
        ref = rows.at[zat(j)] if part is None else rows.at[zat(j), pl.ds(part, 2)]
        return transfer(ref, ref, **where)

    right, left = {"dp": plane(1, 0)}, {"dp": plane(-1, 0)}
    upward, downward = {"dp": plane(0, 1)}, {"dp": plane(0, -1)}
    zp = {i: up_to(0, 1 - i, **upward) for i in (1, 2, 3, 4)}
    zm = {i: up_to(0, i - 1, **downward) for i in (1, 2, 3)}
    around = (0, 1, -1, 2, -2, 3, -3, 4)
    xp = {o: up_to(0, o, **right) for o in around}
    xm = {o: up_to(0, o, **left) for o in around}
    xf = {o: up_to(-1, o, **right) for o in (0, 1, 2, 3)}
    xf.update({o: up_to(1, o, **left) for o in (-1, -2, -3, 4)})

    def rows_about(rows):
        along = [transfer(rows.at[pz, px], rows.at[pz, px], dp=plane(i, 0)) for i in (1, -1, 2)]
        plus = {i: row_to(rows, 1 - i, **upward) for i in (1, 2, 3)}
        minus = {i: row_to(rows, i - 1, **downward) for i in (1, 2, 3)}
        plus[4] = row_to(rows, -3, 0, **upward)
        minus[4] = row_to(rows, 3, 2, **downward)
        return along, plus, minus

    ox, op, om = rows_about(projs)
    bx, bp, bm = rows_about(downs)

    def w1():
        arrive(*first)
        begin(zp[1], zm[1], xp[0], xm[0])
        arrive(*second)
        begin(*ox, *bx)

    def w2():
        arrive(zp[1], zm[1])
        begin(zp[2], zm[2], xp[-1], xm[-1], xp[1], xm[1])

    def w3():
        arrive(*ox)
        begin(op[1], om[1])
        arrive(*bx)
        begin(bp[1], bm[1])

    def w4():
        arrive(zp[2], zm[2])
        arrive(op[1], om[1])
        begin(op[2], om[2])
        begin(zp[3], zm[3], xp[-2], xm[-2], xp[2], xm[2])

    def w5():
        arrive(xp[0])
        begin(xf[0])

    def w6():
        arrive(zp[3], zm[3])
        arrive(op[2], om[2])
        begin(op[3], om[3])
        begin(zp[4], xp[-3], xm[-3], xp[3], xm[3])

    def w7():
        arrive(bp[1], bm[1])
        begin(bp[2], bm[2])

    def w8():
        arrive(zp[4])
        begin(xp[4], xm[4])
        arrive(op[3], om[3])
        begin(op[4], om[4])

    def w9():
        arrive(xp[1], xm[-1])
        begin(xf[1], xf[-1])

    def w10():
        arrive(bp[2], bm[2])
        begin(bp[3], bm[3])

    def w11():
        arrive(xp[2], xm[-2])
        begin(xf[2], xf[-2])

    def w12():
        arrive(xp[3], xm[-3])
        begin(xf[3], xf[-3])

    def w13():
        arrive(bp[3], bm[3])
        begin(bp[4], bm[4])

    def w14():
        arrive(xm[4])
        begin(xf[4])

    def w15():
        arrive(xm[0], xm[1], xp[-1], xm[2], xp[-2], xm[3], xp[-3], xp[4])
        arrive(*xf.values())
        arrive(bp[4], bm[4])

    acc[...] = jnp.zeros_like(acc)
    top[...] = jnp.full_like(top, LOW)
    vt[:, HEAD:, :] = jnp.ones((2, 16, KEYS), bf16)
    qt[...] = jnp.zeros_like(qt)

    w1()
    arrive(*q_out.values())

    def prepare(i, carry):
        y = jnp.transpose(qland[i].astype(f32) * (HEAD**-0.5)).astype(bf16)
        qt[i, 0:HEAD, 0:ROWS] = y[0:HEAD]
        qt[i, 0:HEAD, ROWS:] = y[HEAD:]
        return carry

    lax.fori_loop(0, CHIPS, prepare, 0)

    def process(d):
        near = chip(-d)
        for h in (0, 1):
            for r in range(0, KEYS, 128):
                block = jnp.transpose(kvland[h, d, r : r + 128, :].astype(f32))
                vt[h, 0:HEAD, r : r + 128] = block[HEAD:, :].astype(bf16)

        def shift(i, scores):
            old = top[i]
            new = jnp.maximum(old, jnp.max(scores, axis=0, keepdims=True))
            top[i] = new
            return new, jnp.exp(old - new)

        scores = jnp.dot(kvland[0, d, 0:ROWS, :], qt[near], preferred_element_type=f32)
        key_row = lax.broadcasted_iota(jnp.int32, (ROWS, 2 * ROWS), 0)
        query_row = lax.rem(lax.broadcasted_iota(jnp.int32, (ROWS, 2 * ROWS), 1), ROWS)
        scores = jnp.where(key_row <= query_row, scores, LOW)
        new, shrink = shift(near, scores)
        probs = jnp.where(key_row <= query_row, jnp.exp(scores - new), 0.0).astype(bf16)
        acc[near] = acc[near] * shrink + jnp.dot(vt[0, :, 0:ROWS], probs, preferred_element_type=f32)

        def before(m, carry):
            sa[...] = jnp.dot(kvland[1, d], qt[near], preferred_element_type=f32)
            new, shrink = shift(near, sa[...])
            pa[...] = jnp.exp(sa[...] - new).astype(bf16)
            acc[near] = acc[near] * shrink + jnp.dot(vt[1], pa[...], preferred_element_type=f32)
            return carry

        lax.fori_loop(0, k, before, 0)

        def score(i, h, scores):
            scores[...] = jnp.dot(kvland[h, d], qt[i], preferred_element_type=f32)

        def soften(i, scores, probs, shrink):
            new, shrink[...] = shift(i, scores[...])
            probs[...] = jnp.exp(scores[...] - new).astype(bf16)

        def add(i, h, probs, shrink):
            acc[i] = acc[i] * shrink[...] + jnp.dot(vt[h], probs[...], preferred_element_type=f32)

        score(near + 1, 0, sa)
        soften(near + 1, sa, pa, aa)
        score(near + 1, 1, sb)

        def step(m, carry):
            i = near + 1 + m
            score(i + 1, 0, sa)
            soften(i, sb, pb, ab)
            add(i, 0, pa, aa)
            score(i + 1, 1, sb)
            soften(i + 1, sa, pa, aa)
            add(i, 1, pb, ab)
            return carry

        lax.fori_loop(0, CHIPS - 1 - near, step, 0)

    def pass_on(d):
        arrive(kv_out[d])
        begin(kv_on[d])

    def fold(d):
        arrive(kv_on[d])
        process(d)

    fold(0)
    w2()
    pass_on(1)
    begin(kv_out[3], kv_out[5])
    w3()
    pass_on(7)
    fold(1)
    w5()
    w4()
    pass_on(2)
    begin(kv_out[4])
    fold(7)
    pass_on(6)
    fold(2)
    w6()
    fold(6)
    w7()
    w8()
    w9()
    pass_on(3)
    pass_on(5)
    fold(3)
    pass_on(4)
    fold(5)
    w10()
    w11()
    fold(4)
    w12()

    def finish(i):
        ctx = acc[i, 0:HEAD, :] / acc[i, HEAD : HEAD + 1, :]
        ctx = jnp.concatenate([ctx[:, 0:ROWS], ctx[:, ROWS:]], axis=0)
        return jnp.transpose(ctx).astype(bf16)

    c_out = {d: transfer(cbuf.at[d], cland.at[:, chip_columns(c)], seq=peer(d)) for d in OFFSETS}
    for d in OFFSETS:
        cbuf[d] = finish(chip(d))
        begin(c_out[d])
    cland[:, chip_columns(c)] = finish(c)

    arrive(op[4], om[4])
    for i in range(CHIPS):
        for j in range(ZS):
            block = projs[j, :, i // 4, :, 128 * (i % 4) : 128 * (i % 4) + 128]
            weight[i, k, :, 128 * j : 128 * j + 128] = block.reshape(HEAD, 128)
    w_on = transfer(weight.at[:, k], weight.at[:, k], seq=sib)
    begin(w_on)
    w13()
    arrive(w_on)
    arrive(*c_out.values())
    w14()

    hidden = (
        residual[...].astype(f32)
        + jnp.dot(cland[...], weight[...].reshape(1024, 1024), preferred_element_type=f32)
    ).astype(bf16)
    hid[...] = hidden
    wide = hidden.astype(f32)
    normed = wide * lax.rsqrt(jnp.mean(wide * wide, axis=-1, keepdims=True) + 1e-05) * gain[...]
    x[0:ROWS, :] = normed.astype(bf16)
    x_on = transfer(x.at[pl.ds(0, ROWS)], x.at[pl.ds(ROWS, ROWS)], seq=sib)
    begin(x_on)
    arrive(x_on, gate_on)
    w15()

    def expert(e, up, low, high):
        projected = jnp.dot(x[...], up, preferred_element_type=f32)
        gate, lift = projected[:, :FF], projected[:, FF:]
        column = lax.broadcasted_iota(jnp.int32, (2 * ROWS, 128), 1)
        scale = jnp.sum(jnp.where(column == e, gates[...], 0.0), axis=1, keepdims=True)
        act = (gate / (1.0 + jnp.exp(-gate)) * lift * scale).astype(bf16)
        return (
            jnp.dot(act, low, preferred_element_type=f32),
            jnp.dot(act, high, preferred_element_type=f32),
        )

    up_copy.wait()
    down_copy.wait()
    low, high = expert(s, own_up[...], own_down[:, 0:512], own_down[:, 512:])
    total[:, 0:512] = low
    total[:, 512:] = high

    def other(j, carry):
        low, high = expert(
            chip(j + 1) * 2 + k,
            ups[:, j].reshape(1024, 512),
            downs[0:4, :, j].reshape(FF, 512),
            downs[4:8, :, j].reshape(FF, 512),
        )
        total[:, 0:512] += low
        total[:, 512:] += high
        return carry

    lax.fori_loop(0, CHIPS - 1, other, 0)
    y_on = transfer(total.at[pl.ds(ROWS, ROWS)], yland, seq=sib)
    begin(y_on)
    arrive(y_on)
    out[...] = (hid[...].astype(f32) + total[0:ROWS, :] + yland[...]).astype(bf16)
    for copy in sent:
        copy.wait_send()


def body(
    queries, keyvals, residual, out_weight, norm_gain, expert_up, expert_down, expert_ids, slot_index, gate_weights
):
    dma = pltpu.SemaphoreType.DMA
    vmem = pl.BlockSpec(memory_space=pltpu.VMEM)
    hbm = pl.BlockSpec(memory_space=pl.ANY)
    f32, bf16 = jnp.float32, jnp.bfloat16
    return pl.pallas_call(
        layer_kernel,
        out_shape=jax.ShapeDtypeStruct((ROWS, 1024), bf16),
        in_specs=[hbm, vmem, vmem, vmem, vmem, hbm, hbm, vmem, vmem],
        out_specs=vmem,
        scratch_shapes=[
            pltpu.VMEM((2, CHIPS, KEYS, 128), bf16),
            pltpu.VMEM((CHIPS, ROWS, 128), bf16),
            pltpu.VMEM((CHIPS + 1, 128, 2 * ROWS), bf16),
            pltpu.VMEM((2, HEAD + 16, KEYS), bf16),
            pltpu.VMEM((CHIPS + 1, HEAD + 16, 2 * ROWS), f32),
            pltpu.VMEM((CHIPS + 1, 1, 2 * ROWS), f32),
            pltpu.VMEM((KEYS, 2 * ROWS), f32),
            pltpu.VMEM((KEYS, 2 * ROWS), f32),
            pltpu.VMEM((KEYS, 2 * ROWS), bf16),
            pltpu.VMEM((KEYS, 2 * ROWS), bf16),
            pltpu.VMEM((1, 2 * ROWS), f32),
            pltpu.VMEM((1, 2 * ROWS), f32),
            pltpu.VMEM((CHIPS, ROWS, 128), bf16),
            pltpu.VMEM((ROWS, 1024), bf16),
            pltpu.VMEM((1024, 512), bf16),
            pltpu.VMEM((FF, 1024), bf16),
            pltpu.VMEM((XS * ZS, CHIPS - 1, 32, 512), bf16),
            pltpu.VMEM((ZS, XS, CHIPS - 1, 16, 512), bf16),
            pltpu.VMEM((ZS, XS, 2, 16, 512), bf16),
            pltpu.VMEM((CHIPS, 2, HEAD, 1024), bf16),
            pltpu.VMEM((2 * ROWS, 128), f32),
            pltpu.VMEM((2 * ROWS, 1024), bf16),
            pltpu.VMEM((ROWS, 1024), bf16),
            pltpu.VMEM((2 * ROWS, 1024), f32),
            pltpu.VMEM((ROWS, 1024), f32),
            dma,
            dma,
            dma,
            dma((TRANSFERS,)),
            dma((TRANSFERS,)),
        ],
        compiler_params=pltpu.CompilerParams(
            collective_id=0, has_side_effects=True, vmem_limit_bytes=56 * 1024 * 1024
        ),
        cost_estimate=pl.CostEstimate(flops=60_000_000_000, bytes_accessed=100_000_000, transcendentals=16_000_000),
    )(
        keyvals.transpose(1, 0, 2), queries, residual, out_weight, norm_gain[None], expert_up, expert_down,
        expert_ids.T, gate_weights.T,
    )


def solution(mesh):
    rows = P(("dp", "seq"), None)
    placed = (
        rows,
        P(("dp", "seq"), None, None),
        rows,
        P("seq", None),
        P(),
        P("seq", None, None),
        P("seq", None, None),
        rows,
        rows,
        rows,
    )
    return jax.shard_map(body, mesh=mesh, in_specs=placed, out_specs=rows, check_vma=False)
```

time: 134 us -> 122 us (0.910)
  Pallas kernels: 126 us -> 117 us
  local copies, waits for them, and re-layouts: 7.7 us -> 4.88 us
    pallas_call x1, Pallas kernels: 126 us -> 117 us  [body(): pl.pallas_call(layer_kernel, out_shape=jax.ShapeDtypeStruct((ROWS, 1024),...]
    unnamed x4 -> x2, local copies, waits for them, and re-layouts: 7.7 us -> 4.88 us
where the time goes in v3:
time: 122 us
  Pallas kernels  117 us (96%)
  local copies, waits for them, and re-layouts  4.88 us (4%)
    pallas_call x1, Pallas kernels, body(): pl.pallas_call(layer_kernel, out_shape=jax.ShapeDtypeStruct((ROWS, 1024),...  117 us
    unnamed x2, local copies, waits for them, and re-layouts  4.88 us

profile of v3, /device:TPU:1, one launch (start us, length us, event | category | flops | bytes accessed | tf_op | source)
XLA Modules:
  0.0 122.0 jit_solution(17023524232923363211)
XLA Ops:
  0.0 3.2 %copy.12 = bf16[1024,8,128]{2,0,1:T(8,128)(2,1)} copy(bf16[1024,8,128]{2,1,0:T(8,128)(2,1)} %param.11) | data formatting | bytes 4194304 | tf_op args[1]
  3.2 117.1 %shard_map.91 = bf16[128,1024]{1,0:T(8,128)(2,1)} custom-call(bf16[8,1024,128]{2,1,0:T(8,128)(2,1)} %bitcast.6, bf16[128,1024]{1,0:T(8,128)(2,1)} %q.1, bf16[128,1024]{1,0:T(8,128)(2,1)} %residual.1, bf16[64,1024]{1,0:T(8,128)(2,1)} %proj.1, f32[1,1024]{1,0:T(1,128)} %bitcast.7, bf16[1,1024,512]{2,1,0:T(8,128)(2,1)} %up_in.1, bf16[1,256,1024]{2,1,0:T(8,128)(2,1)} %down_in.1, ...), custom_call_target="tpu_custom_call" | custom-call | flops 60000002048 | bytes 100000000 | tf_op jit(solution)/shard_map/pallas_call | solution.py:416
  120.3 1.7 %copy.14 = bf16[128,1024]{1,0:T(8,128)(2,1)} copy(bf16[128,1024]{1,0:T(8,128)(2,1)} %shard_map.91) | data formatting | bytes 524288

commit v4 on v3

--- a/solution.py
+++ b/solution.py
@@ -114,14 +114,14 @@
                 seq=peer(d),
             )
         )
-    begin(*first, *second)
+    begin(*first)
 
     q_out = {d: transfer(q.at[:, chip_columns(chip(d))], qland.at[c], seq=peer(d)) for d in OFFSETS}
     kv_out = {d: transfer(kv.at[chip(d)], kvland.at[0, d], seq=peer(d)) for d in OFFSETS}
     kv_on = {d: transfer(kvland.at[0, d], kvland.at[1, d], seq=sib) for d in (0,) + OFFSETS}
     gate_on = transfer(gates.at[pl.ds(0, ROWS)], gates.at[pl.ds(ROWS, ROWS)], seq=sib)
     begin(*q_out.values())
-    begin(*[kv_out[d] for d in OFFSETS[:4]])
+    begin(*second)
     own_kv.wait()
     begin(kv_on[0], gate_on)
 
@@ -156,6 +156,7 @@
     def w1():
         arrive(*first)
         begin(zp[1], zm[1], xp[0], xm[0])
+        begin(*[kv_out[d] for d in OFFSETS[:4]])
         arrive(*second)
         begin(*ox, *bx)
 
@@ -327,8 +328,8 @@
     pass_on(5)
     fold(3)
     pass_on(4)
+    w10()
     fold(5)
-    w10()
     w11()
     fold(4)
     w12()
@@ -367,7 +368,6 @@
     x_on = transfer(x.at[pl.ds(0, ROWS)], x.at[pl.ds(ROWS, ROWS)], seq=sib)
     begin(x_on)
     arrive(x_on, gate_on)
-    w15()
 
     def expert(e, up, low, high):
         projected = jnp.dot(x[...], up, preferred_element_type=f32)
@@ -385,6 +385,7 @@
     low, high = expert(s, own_up[...], own_down[:, 0:512], own_down[:, 512:])
     total[:, 0:512] = low
     total[:, 512:] = high
+    w15()
 
     def other(j, carry):
         low, high = expert(

time: 122 us -> 123 us (level)
  no operation moved by 1% of the time
where the time goes in v4:
time: 123 us
  Pallas kernels  118 us (96%)
  local copies, waits for them, and re-layouts  4.88 us (4%)
    pallas_call x1, Pallas kernels, body(): pl.pallas_call(layer_kernel, out_shape=jax.ShapeDtypeStruct((ROWS, 1024),...  118 us
    unnamed x2, local copies, waits for them, and re-layouts  4.88 us

profile of v4, /device:TPU:1, one launch (start us, length us, event | category | flops | bytes accessed | tf_op | source)
XLA Modules:
  0.0 123.0 jit_solution(6679465812808605115)
XLA Ops:
  0.0 3.2 %copy.12 = bf16[1024,8,128]{2,0,1:T(8,128)(2,1)} copy(bf16[1024,8,128]{2,1,0:T(8,128)(2,1)} %param.11) | data formatting | bytes 4194304 | tf_op args[1]
  3.2 118.1 %shard_map.91 = bf16[128,1024]{1,0:T(8,128)(2,1)} custom-call(bf16[8,1024,128]{2,1,0:T(8,128)(2,1)} %bitcast.6, bf16[128,1024]{1,0:T(8,128)(2,1)} %q.1, bf16[128,1024]{1,0:T(8,128)(2,1)} %residual.1, bf16[64,1024]{1,0:T(8,128)(2,1)} %proj.1, f32[1,1024]{1,0:T(1,128)} %bitcast.7, bf16[1,1024,512]{2,1,0:T(8,128)(2,1)} %up_in.1, bf16[1,256,1024]{2,1,0:T(8,128)(2,1)} %down_in.1, ...), custom_call_target="tpu_custom_call" | custom-call | flops 60000002048 | bytes 100000000 | tf_op jit(solution)/shard_map/pallas_call | solution.py:417
  121.4 1.7 %copy.14 = bf16[128,1024]{1,0:T(8,128)(2,1)} copy(bf16[128,1024]{1,0:T(8,128)(2,1)} %shard_map.91) | data formatting | bytes 524288
